TPU v7x, 256 devices: a whole 4x4x8 slice. The times are simulated.
256 devices in a mesh: outer: 64 (over y_lo, z, x), inner: 4 (over y_hi, core).
Axes of the slice: x: 4, y: 4 (y_hi: 2, y_lo: 2; y = y_hi * 2 + y_lo), z: 8, core: 2. Of those that a mesh axis runs over, the one named last changes fastest.
Arguments:
- frames: bfloat16 [32768, 1024], P(('outer', 'inner')), may hold values from -6 to 6
- gain_attn: float32 [1024], replicated, may hold values from 0.5 to 2
- w_query: bfloat16 [1024, 512], replicated, may hold values from -4 to 4
- w_key: bfloat16 [1024, 512], replicated, may hold values from -0.1875 to 0.1875
- w_value: bfloat16 [1024, 512], replicated, may hold values from -0.1875 to 0.1875
- w_out: bfloat16 [512, 1024], replicated, may hold values from -0.25 to 0.25
- gain_conv: float32 [1024], replicated, may hold values from 0.5 to 2
- w_expand: bfloat16 [1024, 2048], replicated, may hold values from -0.1875 to 0.1875
- kernel_taps: float32 [31, 1024], replicated, may hold values from -2 to 2
- bn_scale: float32 [1024], replicated, may hold values from 0.5 to 2
- bn_shift: float32 [1024], replicated, may hold values from -3 to 3
- w_project: bfloat16 [1024, 1024], replicated, may hold values from -0.1875 to 0.1875
Outputs:
- block_out: bfloat16 [32768, 1024], P(('outer', 'inner'))
All inputs are finite; a program needn't handle non-finite values.
Results may differ from a plain program's by a relative error of at most 0.017.
The roundings to bfloat16 on the way count: a program that leaves them out, or rounds other values in their place, can miss the bound.
Values may be sent and summed in bfloat16 or wider, within the bound.
No kernel may reach another device: no remote copies, remote signals or barrier semaphores. Data moves between devices by JAX's collectives and lax.ppermute only.
A program may use at most 128 MiB of HBM per device.

v0:
```python
import jax
import jax.numpy as jnp
from jax import lax
from jax.sharding import PartitionSpec as P

HEAD_DIM = 64


def with_halo(cells, sides, width):
    for axis, dim in sides:
        count = lax.axis_size(axis)
        ends = count - 1
        head = lax.slice_in_dim(cells, 0, width, axis=dim)
        tail = lax.slice_in_dim(cells, cells.shape[dim] - width, cells.shape[dim], axis=dim)
        cells = jnp.concatenate(
            [
                lax.ppermute(tail, axis, [(i, (i + 1) % count) for i in range(ends)]),
                cells,
                lax.ppermute(head, axis, [((i + 1) % count, i) for i in range(ends)]),
            ],
            axis=dim,
        )
    return cells


def norm_rows(values, gain):
    values = values.astype(jnp.float32)
    center = values - jnp.mean(values, axis=-1, keepdims=True)
    spread = jnp.mean(center * center, axis=-1, keepdims=True)
    return center * lax.rsqrt(spread + 1e-05) * gain


def attend_update(carry, query_heads, key_piece, value_piece, scale):
    rows = key_piece.shape[0]
    head_count = query_heads.shape[1]
    head_size = query_heads.shape[2]
    block = 512
    key_blocks = key_piece.reshape(rows // block, block, head_count, head_size)
    value_blocks = value_piece.reshape(rows // block, block, head_count, head_size)

    def one_block(state, pair):
        accum, top, total = state
        key_block, value_block = pair
        scores = (
            jnp.einsum("qhd,khd->qhk", query_heads, key_block, preferred_element_type=jnp.float32)
            * scale
        )
        new_top = jnp.maximum(top, jnp.max(scores, axis=-1))
        factor = jnp.exp(top - new_top)
        weights = jnp.exp(scores - new_top[:, :, None])
        total = total * factor + jnp.sum(weights, axis=-1)
        mixed = jnp.einsum(
            "qhk,khd->qhd",
            weights.astype(jnp.bfloat16),
            value_block,
            preferred_element_type=jnp.float32,
        )
        accum = accum * factor[:, :, None] + mixed
        return ((accum, new_top, total), None)

    carry, unused = lax.scan(one_block, carry, (key_blocks, value_blocks))
    return carry


def body(
    frames,
    gain_attn,
    w_query,
    w_key,
    w_value,
    w_out,
    gain_conv,
    w_expand,
    kernel_taps,
    bn_scale,
    bn_shift,
    w_project,
):
    own_rows = frames.shape[0]
    model_width = frames.shape[1]
    group = lax.axis_size("inner")
    head_size = HEAD_DIM
    width = w_query.shape[1]
    local_width = width // group
    local_heads = local_width // head_size
    scale = head_size ** (-0.5)
    normed = norm_rows(frames, gain_attn).astype(jnp.bfloat16)
    start_col = lax.axis_index("inner") * local_width
    chosen = jnp.concatenate(
        [
            lax.dynamic_slice_in_dim(w_query, start_col, local_width, 1),
            lax.dynamic_slice_in_dim(w_key, start_col, local_width, 1),
            lax.dynamic_slice_in_dim(w_value, start_col, local_width, 1),
        ],
        axis=1,
    )
    projected = jnp.dot(
        lax.all_gather(normed, "inner", axis=0, tiled=True),
        chosen,
        preferred_element_type=jnp.float32,
    ).astype(jnp.bfloat16)
    query_local = projected[:, :local_width]
    key_local = projected[:, local_width : 2 * local_width]
    value_local = projected[:, 2 * local_width :]
    block_rows = group * own_rows
    query_heads = query_local.reshape(block_rows, local_heads, head_size)
    start_state = (
        jnp.zeros((block_rows, local_heads, head_size), jnp.float32),
        jnp.full((block_rows, local_heads), -jnp.inf, jnp.float32),
        jnp.zeros((block_rows, local_heads), jnp.float32),
    )
    final_state = attend_update(
        start_state,
        query_heads,
        lax.all_gather(key_local, "outer", axis=0, tiled=True),
        lax.all_gather(value_local, "outer", axis=0, tiled=True),
        scale,
    )
    accum, top, total = final_state
    context_local = (
        (accum / total[:, :, None]).astype(jnp.bfloat16).reshape(block_rows, 1, local_width)
    )
    returned = lax.all_to_all(context_local, "inner", split_axis=0, concat_axis=1, tiled=True)
    context = returned.reshape(own_rows, width)
    attn = jnp.dot(context, w_out, preferred_element_type=jnp.float32)
    hidden = (frames.astype(jnp.float32) + attn).astype(jnp.bfloat16)
    normed2 = norm_rows(hidden, gain_conv).astype(jnp.bfloat16)
    expand = jnp.dot(normed2, w_expand, preferred_element_type=jnp.float32)
    glu = (expand[:, :model_width] * jax.nn.sigmoid(expand[:, model_width:])).astype(jnp.bfloat16)
    taps = kernel_taps.shape[0]
    half_kernel = taps // 2
    padded = with_halo(glu, ((("outer", "inner"), 0),), half_kernel)
    conv = jnp.zeros((own_rows, model_width), jnp.float32)
    for tap in range(taps):
        conv = conv + kernel_taps[tap] * padded[tap : tap + own_rows].astype(jnp.float32)
    act = jax.nn.silu(bn_scale * conv + bn_shift).astype(jnp.bfloat16)
    result = hidden.astype(jnp.float32) + jnp.dot(
        act, w_project, preferred_element_type=jnp.float32
    )
    return result.astype(jnp.bfloat16)


def solution(mesh):
    return jax.shard_map(
        body,
        mesh=mesh,
        in_specs=(
            P(("outer", "inner"), None),
            P(),
            P(),
            P(),
            P(),
            P(),
            P(),
            P(),
            P(),
            P(),
            P(),
            P(),
        ),
        out_specs=P(("outer", "inner"), None),
        check_vma=False,
    )
```

profile of v0, /device:TPU:1, one launch (start us, length us, event | category | flops | bytes accessed | tf_op | source)
XLA Modules:
  0.0 1131.6 jit_solution(17595431488501985609)
XLA Ops:
  13.0 25.6 %all-gather.4.cloned.1.call-done = bf16[512,1024]{1,0:T(8,128)(2,1)} async-done(((bf16[128,1024]{1,0:T(8,128)(2,1)}), bf16[512,1024]{1,0:T(8,128)(2,1)}) %all-gather.4.cloned.1.call-update) | async-done | bytes 1048592 | tf_op jit(solution)/shard_map/all_gather | solution.py:98
  41.9 269.5 %all-gather.6.cloned.1.call-done = bf16[32768,128]{0,1:T(8,128)(2,1)} async-done(((bf16[512,128]{0,1:T(8,128)(2,1)}), bf16[32768,128]{0,1:T(8,128)(2,1)}) %all-gather.6.cloned.1.call-update) | async-done | bytes 8388624 | tf_op jit(solution)/shard_map/all_gather | solution.py:115
  311.4 10.1 copy.36
  321.6 11.3 %copy.30 = bf16[64,512,2,64]{1,3,2,0:T(8,128)(2,1)} copy(bf16[64,512,2,64]{1,0,3,2:T(8,128)(2,1)} %bitcast.89) | data formatting | bytes 16777216
  332.9 289.6 %all-gather.8.cloned.1.call-done = bf16[32768,128]{0,1:T(8,128)(2,1)} async-done(((bf16[512,128]{0,1:T(8,128)(2,1)}), bf16[32768,128]{0,1:T(8,128)(2,1)}) %all-gather.8.cloned.1.call-update) | async-done | bytes 8388624 | tf_op jit(solution)/shard_map/all_gather | solution.py:116
  622.5 10.3 copy.37
  632.8 11.4 %copy.31 = bf16[64,512,2,64]{1,3,2,0:T(8,128)(2,1)} copy(bf16[64,512,2,64]{1,0,3,2:T(8,128)(2,1)} %bitcast.90) | data formatting | bytes 16777216
  644.2 409.9 %while.15 = (s32[]{:T(128)}, f32[512,2,64]{0,2,1:T(8,128)S(1)}, f32[512,2]{0,1:T(2,128)S(1)}, f32[512,2]{0,1:T(2,128)S(1)}, bf16[64,512,2,64]{1,3,2,0:T(8,128)(2...) while((s32[]{:T(128)}, f32[512,2,64]{0,2,1:T(8,128)S(1)}, ...), condition=%wide.region_5.6_spmd.clone, body=%wide.region_2.5_spmd.clone.sunk | while | flops 138613760 | bytes 15664261 | solution.py:61
  644.2 2.8 bitcast_reduce_fusion.2
  650.6 2.7 bitcast_reduce_fusion.2
  663.4 2.7 bitcast_reduce_fusion.2
  676.2 2.7 bitcast_reduce_fusion.2
  689.0 2.7 bitcast_reduce_fusion.2
  701.9 2.7 bitcast_reduce_fusion.2
  714.7 2.7 bitcast_reduce_fusion.2
  727.5 2.7 bitcast_reduce_fusion.2
  740.3 2.7 bitcast_reduce_fusion.2
  881.2 2.7 bitcast_reduce_fusion.2
  1056.1 45.4 %all-to-all-start = ((bf16[4,2,8192]{2,1,0:T(2,128)(2,1)}), bf16[4,2,8192]{2,1,0:T(2,128)(2,1)S(1)}, u32[]{:S(2)}, u32[]{:S(2)}) async-start(bf16[4,2,8192]{2,1,0:T(2,128)(2,1)} %reshape.52), calls=%async_computation | async-start | bytes 262144 | tf_op jit(solution)/shard_map/all_to_all | solution.py:123
  1101.6 5.0 all-to-all-done
  1108.9 3.0 fusion.35
  1112.0 2.9 collective-permute-start
  1116.9 4.8 collective-permute-done.1
  1121.7 3.4 fusion.19
  (550 shorter events, 396.2 us)
Async XLA Ops:
  6.5 1115.1 %copy-start = (bf16[1024,1024]{1,0:T(8,128)(2,1)S(1)}, bf16[1024,1024]{1,0:T(8,128)(2,1)}, u32[]{:S(2)}) copy-start(bf16[1024,1024]{1,0:T(8,128)(2,1)} %param.25) | copy-start | bytes 6291460
  6.5 32.0 %all-gather.4.cloned.1.call-start = ((), (), s32[]{:S(2)}) async-start(), calls=%async_computation.1 | async-start | bytes 1310720 | tf_op jit(solution)/shard_map/all_gather | solution.py:98
  10.9 300.6 %all-gather.6.cloned.1.call-start = ((), (), s32[]{:S(2)}) async-start(), calls=%async_computation.2 | async-start | bytes 8519680 | tf_op jit(solution)/shard_map/all_gather | solution.py:115
  41.1 581.4 %all-gather.8.cloned.1.call-start = ((), (), s32[]{:S(2)}) async-start(), calls=%async_computation.3 | async-start | bytes 8519680 | tf_op jit(solution)/shard_map/all_gather | solution.py:116
  644.2 457.4 %copy-start.3 = (f32[31,1024]{1,0:T(8,128)S(1)}, f32[31,1024]{1,0:T(8,128)}, u32[]{:S(2)}) copy-start(f32[31,1024]{1,0:T(8,128)} %param.22) | copy-start | bytes 380932
  647.0 2.2 copy-start.1
  653.4 2.2 copy-start.1
  659.8 2.2 copy-start.1
  666.2 2.2 copy-start.1
  672.6 2.2 copy-start.1
  679.0 2.2 copy-start.1
  685.4 2.2 copy-start.1
  691.8 2.2 copy-start.1
  698.2 2.2 copy-start.1
  704.6 2.2 copy-start.1
  711.0 2.2 copy-start.1
  717.4 2.2 copy-start.1
  1054.1 52.9 %copy-start.2 = (bf16[128,1024]{1,0:T(8,128)(2,1)S(1)}, bf16[128,1024]{1,0:T(8,128)(2,1)}, u32[]{:S(2)}) copy-start(bf16[128,1024]{1,0:T(8,128)(2,1)} %param.14) | copy-start | bytes 786436
  1055.4 53.4 %copy-start.4 = (f32[1024]{0:T(1024)S(1)}, f32[1024]{0:T(1024)}, u32[]{:S(2)}) copy-start(f32[1024]{0:T(1024)} %param.20) | copy-start | bytes 12292
  1056.1 50.5 %all-to-all-start = ((bf16[4,2,8192]{2,1,0:T(2,128)(2,1)}), bf16[4,2,8192]{2,1,0:T(2,128)(2,1)S(1)}, u32[]{:S(2)}, u32[]{:S(2)}) async-start(bf16[4,2,8192]{2,1,0:T(2,128)(2,1)} %reshape.52), calls=%async_computation | async-start | bytes 262144 | tf_op jit(solution)/shard_map/all_to_all | solution.py:123
  1108.8 12.8 %copy-start.5 = (f32[1024]{0:T(1024)S(1)}, f32[1024]{0:T(1024)}, u32[]{:S(2)}) copy-start(f32[1024]{0:T(1024)} %param.24) | copy-start | bytes 12292
  1108.9 12.8 %copy-start.6 = (f32[1024]{0:T(1024)S(1)}, f32[1024]{0:T(1024)}, u32[]{:S(2)}) copy-start(f32[1024]{0:T(1024)} %param.23) | copy-start | bytes 12292
  1112.0 4.9 collective-permute-start
  1114.9 6.7 collective-permute-start.1
  (52 other events, 115.5 us)
Sparse Core Ops, SparseCore 0:
  11.0 27.5 all-gather.3
  41.3 270.1 all-gather.5
  313.2 309.2 all-gather.7
where the time goes:
time: 1130 us
  waiting for transfers between devices  595 us (53%)
  matrix products  275 us (24%)
  other arithmetic  141 us (12%)
  local copies, waits for them, and re-layouts  53.5 us (5%)
  starting transfers between devices  50.3 us (4%)
  between operations  13.3 us (1%)
    all_gather x1, waiting for transfers between devices, body(): lax.all_gather(value_local, 'outer', axis=0, tiled=True)  290 us
    all_gather x1, waiting for transfers between devices, body(): lax.all_gather(key_local, 'outer', axis=0, tiled=True)  270 us
    dot_general x64, matrix products, one_block(): jnp.einsum('qhd,khd->qhk', query_heads, key_block, preferred_element_type...  175 us
    reduce_sum x64, other arithmetic, one_block(): total = total * factor + jnp.sum(weights, axis=-1)  134 us
    dot_general x64, matrix products, one_block(): jnp.einsum('qhk,khd->qhd', weights.astype(jnp.bfloat16), value_block, pre...  90.4 us
    all_to_all x1, starting transfers between devices, body(): lax.all_to_all(context_local, 'inner', split_axis=0, concat_axis=1, tiled...  45.4 us
    unnamed x20, local copies, waits for them, and re-layouts  44.1 us
    all_gather x1, waiting for transfers between devices, body(): lax.all_gather(normed, 'inner', axis=0, tiled=True)  25.6 us
  transfers between devices with their start and end apart: 6, of which 5 were waited for; matrix products, arithmetic and copies ran while one was open for 2% of the time, Pallas kernels for 0%

commit v1 on v0

--- a/solution.py
+++ b/solution.py
@@ -4,6 +4,18 @@
 from jax.sharding import PartitionSpec as P
 
 HEAD_DIM = 64
+
+
+def _deliver_panel(chunk):
+    return jnp.concatenate(
+        jax.lax.all_to_all(
+            jnp.stack([chunk] * jax.lax.axis_size("outer"), 0),
+            axis_name="outer",
+            split_axis=0,
+            concat_axis=0,
+        ),
+        0,
+    )
 
 
 def with_halo(cells, sides, width):
@@ -112,7 +124,7 @@
     final_state = attend_update(
         start_state,
         query_heads,
-        lax.all_gather(key_local, "outer", axis=0, tiled=True),
+        _deliver_panel(key_local),
         lax.all_gather(value_local, "outer", axis=0, tiled=True),
         scale,
     )

time: 1130 us -> 904 us (0.80)
  waiting for transfers between devices: 595 us -> 383 us
  local copies, waits for them, and re-layouts: 53.5 us -> 36.1 us
    all_gather x1 -> x0, waiting for transfers between devices: 270 us -> none  [body(): lax.all_gather(key_local, 'outer', axis=0, tiled=True)]
    all_gather x1, waiting for transfers between devices: 290 us -> 347 us  [body(): lax.all_gather(value_local, 'outer', axis=0, tiled=True)]
    unnamed x20 -> x18, local copies, waits for them, and re-layouts: 44.1 us -> 22.5 us
    all_to_all x1, starting transfers between devices: 45.4 us -> 33.6 us  [body(): lax.all_to_all(context_local, 'inner', split_axis=0, concat_axis=1, tiled...]
  transfers between devices with their start and end apart: 6 -> 6, of which waited for: 5 -> 4; matrix products, arithmetic and copies ran while one was open for 2% -> 3% of each run, Pallas kernels for 0% -> 0%
where the time goes in v1:
time: 904 us; the launch traced here: 901 us
  waiting for transfers between devices  383 us (42%)
  matrix products  276 us (31%)
  other arithmetic  141 us (16%)
  starting transfers between devices  49.3 us (5%)
  local copies, waits for them, and re-layouts  36.1 us (4%)
  between operations  13.6 us (2%)
    all_gather x1, waiting for transfers between devices, body(): lax.all_gather(value_local, 'outer', axis=0, tiled=True)  347 us
    dot_general x64, matrix products, one_block(): jnp.einsum('qhd,khd->qhk', query_heads, key_block, preferred_element_type...  175 us
    reduce_sum x64, other arithmetic, one_block(): total = total * factor + jnp.sum(weights, axis=-1)  134 us
    dot_general x64, matrix products, one_block(): jnp.einsum('qhk,khd->qhd', weights.astype(jnp.bfloat16), value_block, pre...  90.4 us
    all_to_all x1, starting transfers between devices, body(): lax.all_to_all(context_local, 'inner', split_axis=0, concat_axis=1, tiled...  33.6 us
    all_gather x1, waiting for transfers between devices, body(): lax.all_gather(normed, 'inner', axis=0, tiled=True)  25.6 us
    unnamed x18, local copies, waits for them, and re-layouts  22.5 us
  transfers between devices with their start and end apart: 6, of which 4 were waited for; matrix products, arithmetic and copies ran while one was open for 3% of the time, Pallas kernels for 0%

profile of v1, /device:TPU:1, one launch (start us, length us, event | category | flops | bytes accessed | tf_op | source)
XLA Modules:
  0.0 901.2 jit_solution(15976897597471925591)
XLA Ops:
  13.0 25.6 %all-gather.3.cloned.1.call-done = bf16[512,1024]{1,0:T(8,128)(2,1)} async-done(((bf16[128,1024]{1,0:T(8,128)(2,1)}), bf16[512,1024]{1,0:T(8,128)(2,1)}) %all-gather.3.cloned.1.call-update) | async-done | bytes 1048592 | tf_op jit(solution)/shard_map/all_gather | solution.py:110
  41.1 4.2 stack.2
  45.4 10.6 %all-to-all-start = ((bf16[64,512,128]{1,2,0:T(8,128)(2,1)}), bf16[64,512,128]{1,2,0:T(8,128)(2,1)}, u32[]{:S(2)}, u32[]{:S(2)}) async-start(bf16[64,512,128]{1,2,0:T(8,128)(2,1)} %stack.2), calls=%async_computation | async-start | bytes 16777216 | tf_op jit(solution)/shard_map/all_to_all | solution.py:11
  56.0 347.5 %all-gather.5.cloned.1.call-done = bf16[32768,128]{0,1:T(8,128)(2,1)} async-done(((bf16[512,128]{0,1:T(8,128)(2,1)}), bf16[32768,128]{0,1:T(8,128)(2,1)}) %all-gather.5.cloned.1.call-update) | async-done | bytes 8388624 | tf_op jit(solution)/shard_map/all_gather | solution.py:128
  403.5 10.1 %copy.31 = bf16[16,8,64,512]{3,2,1,0:T(8,128)(2,1)} copy(bf16[16,8,64,512]{3,1,2,0:T(8,128)(2,1)} %bitcast.86) | data formatting | bytes 16777216
  413.6 11.3 %copy.26 = bf16[64,512,2,64]{1,3,2,0:T(8,128)(2,1)} copy(bf16[64,512,2,64]{1,0,3,2:T(8,128)(2,1)} %bitcast.85) | data formatting | bytes 16777216
  425.0 410.2 %while.15 = (s32[]{:T(128)}, f32[512,2,64]{0,2,1:T(8,128)S(1)}, f32[512,2]{0,1:T(2,128)S(1)}, f32[512,2]{0,1:T(2,128)S(1)}, bf16[64,512,2,64]{1,3,2,0:T(8,128)(2...) while((s32[]{:T(128)}, f32[512,2,64]{0,2,1:T(8,128)S(1)}, ...), condition=%wide.region_5.6_spmd.clone, body=%wide.region_2.5_spmd.clone.sunk | while | flops 138613760 | bytes 15664261 | solution.py:73
  425.0 2.8 bitcast_reduce_fusion.2
  437.8 2.7 bitcast_reduce_fusion.2
  444.2 2.7 bitcast_reduce_fusion.2
  501.9 2.7 bitcast_reduce_fusion.2
  540.4 2.7 bitcast_reduce_fusion.2
  546.8 2.7 bitcast_reduce_fusion.2
  604.5 2.7 bitcast_reduce_fusion.2
  642.9 2.7 bitcast_reduce_fusion.2
  649.3 2.7 bitcast_reduce_fusion.2
  694.2 2.7 bitcast_reduce_fusion.2
  700.6 2.7 bitcast_reduce_fusion.2
  837.3 33.6 %all-to-all-start.1 = ((bf16[4,2,8192]{2,1,0:T(2,128)(2,1)}), bf16[4,2,8192]{2,1,0:T(2,128)(2,1)S(1)}, u32[]{:S(2)}, u32[]{:S(2)}) async-start(bf16[4,2,8192]{2,1,0:T(2,128)(2,1)} %reshape.50), calls=%async_computation.1 | async-start | bytes 262144 | tf_op jit(solution)/shard_map/all_to_all | solution.py:135
  870.9 5.0 all-to-all-done.1
  878.2 3.0 fusion.35
  881.3 2.9 collective-permute-start
  886.5 4.5 collective-permute-done.1
  891.0 3.4 fusion.19
  (548 shorter events, 393.2 us)
Async XLA Ops:
  6.5 884.5 %copy-start = (bf16[1024,1024]{1,0:T(8,128)(2,1)S(1)}, bf16[1024,1024]{1,0:T(8,128)(2,1)}, u32[]{:S(2)}) copy-start(bf16[1024,1024]{1,0:T(8,128)(2,1)} %param.25) | copy-start | bytes 6291460
  6.5 32.0 %all-gather.3.cloned.1.call-start = ((), (), s32[]{:S(2)}) async-start(), calls=%async_computation.2 | async-start | bytes 1310720 | tf_op jit(solution)/shard_map/all_gather | solution.py:110
  10.9 392.6 %all-gather.5.cloned.1.call-start = ((), (), s32[]{:S(2)}) async-start(), calls=%async_computation.3 | async-start | bytes 8519680 | tf_op jit(solution)/shard_map/all_gather | solution.py:128
  45.4 379.6 %all-to-all-start = ((bf16[64,512,128]{1,2,0:T(8,128)(2,1)}), bf16[64,512,128]{1,2,0:T(8,128)(2,1)}, u32[]{:S(2)}, u32[]{:S(2)}) async-start(bf16[64,512,128]{1,2,0:T(8,128)(2,1)} %stack.2), calls=%async_computation | async-start | bytes 16777216 | tf_op jit(solution)/shard_map/all_to_all | solution.py:11
  425.0 445.9 %copy-start.3 = (f32[31,1024]{1,0:T(8,128)S(1)}, f32[31,1024]{1,0:T(8,128)}, u32[]{:S(2)}) copy-start(f32[31,1024]{1,0:T(8,128)} %param.22) | copy-start | bytes 380932
  427.7 2.2 copy-start.1
  434.2 2.2 copy-start.1
  440.6 2.2 copy-start.1
  447.0 2.2 copy-start.1
  453.4 2.2 copy-start.1
  459.8 2.2 copy-start.1
  466.2 2.2 copy-start.1
  472.6 2.2 copy-start.1
  485.4 2.2 copy-start.1
  504.7 2.2 copy-start.1
  511.1 2.2 copy-start.1
  517.5 2.2 copy-start.1
  835.2 41.1 %copy-start.2 = (bf16[128,1024]{1,0:T(8,128)(2,1)S(1)}, bf16[128,1024]{1,0:T(8,128)(2,1)}, u32[]{:S(2)}) copy-start(bf16[128,1024]{1,0:T(8,128)(2,1)} %param.14) | copy-start | bytes 786436
  836.6 41.6 %copy-start.4 = (f32[1024]{0:T(1024)S(1)}, f32[1024]{0:T(1024)}, u32[]{:S(2)}) copy-start(f32[1024]{0:T(1024)} %param.20) | copy-start | bytes 12292
  837.3 38.7 %all-to-all-start.1 = ((bf16[4,2,8192]{2,1,0:T(2,128)(2,1)}), bf16[4,2,8192]{2,1,0:T(2,128)(2,1)S(1)}, u32[]{:S(2)}, u32[]{:S(2)}) async-start(bf16[4,2,8192]{2,1,0:T(2,128)(2,1)} %reshape.50), calls=%async_computation.1 | async-start | bytes 262144 | tf_op jit(solution)/shard_map/all_to_all | solution.py:135
  878.1 12.8 %copy-start.5 = (f32[1024]{0:T(1024)S(1)}, f32[1024]{0:T(1024)}, u32[]{:S(2)}) copy-start(f32[1024]{0:T(1024)} %param.24) | copy-start | bytes 12292
  878.2 12.8 %copy-start.6 = (f32[1024]{0:T(1024)S(1)}, f32[1024]{0:T(1024)}, u32[]{:S(2)}) copy-start(f32[1024]{0:T(1024)} %param.23) | copy-start | bytes 12292
  881.3 5.1 collective-permute-start
  884.2 6.7 collective-permute-start.1
  (52 other events, 115.5 us)
Sparse Core Ops, SparseCore 0:
  11.0 27.5 all-gather.2
  41.2 362.2 all-gather.4
